TPU v7x, 32 devices: a whole 2x2x4 slice. The times are simulated.
32 devices in a mesh: subj: 4 (over x, core), space: 8 (over z, y).
Axes of the slice: x: 2, y: 2, z: 4, core: 2. Of those that a mesh axis runs over, the one named last changes fastest.
Arguments:
- images: bfloat16 [8, 512, 16, 128], P('subj', 'space'), may hold values from -6 to 6
- velocity: float32 [3, 8, 512, 16, 128], P(None, 'subj', 'space'), may hold values from -4 to 4
- weights: bfloat16 [3, 8, 512, 16, 128], P(None, 'subj', 'space'), may hold values from 0 to 1
- template: float32 [512, 16, 128], P('space', 'subj'), may hold values from -6 to 6
- owners: int32 [8, 512, 1], P('subj', 'space'), may hold values from 0 to 7; in each aligned block of 64 rows (0 to 63, 64 to 127, ..., all dimensions but the last counted through in order) at most 16 rows name the same one
- local_rows: int32 [8, 512], P('subj', 'space'), may hold values from 0 to 63
- tile_counts: int32 [8, 8], P('subj', 'space'), may hold values from 32 to 64
Outputs:
- new_velocity: float32 [3, 8, 512, 16, 128], P(None, 'subj', 'space')
- new_template: float32 [512, 16, 128], P('space', 'subj')
Inputs may be any that keep to these rules, and one draw needn't show every extreme that they name: `owners`: for each subject and each aligned block of 64 tiles, no value appears more than 16 times, and some value appears exactly 16 times.
All inputs are finite; a program needn't handle non-finite values.
Results may differ from a plain program's by a relative error of at most 0.0006.
Values may be sent and summed in bfloat16 or wider, within the bound.
No kernel may reach another device: no remote copies, remote signals or barrier semaphores. Data moves between devices by JAX's collectives and lax.ppermute only.
A program may use at most 64 MiB of HBM per device.

v0:
```python
import jax
import jax.numpy as jnp
from jax import lax
from jax.sharding import PartitionSpec as P

BX = 4
BY = 4
ITERS = 2


ridge = 0.25


def extended(block, sides, width):
    for axis, dim in sides:
        count = lax.axis_size(axis)
        forward = [(i, i + 1) for i in range(count - 1)]
        backward = [(target, source) for source, target in forward]
        low = lax.ppermute(
            lax.slice_in_dim(block, block.shape[dim] - width, None, axis=dim), axis, forward
        )
        high = lax.ppermute(lax.slice_in_dim(block, 0, width, axis=dim), axis, backward)
        block = jnp.concatenate([low, block, high], axis=dim)
    return block


def shift_up(field, axis):
    body_part = lax.slice_in_dim(field, 1, field.shape[axis], axis=axis)
    edge = jnp.zeros_like(lax.slice_in_dim(field, 0, 1, axis=axis))
    return jnp.concatenate([body_part, edge], axis)


def shift_down(field, axis):
    body_part = lax.slice_in_dim(field, 0, field.shape[axis] - 1, axis=axis)
    edge = jnp.zeros_like(lax.slice_in_dim(field, 0, 1, axis=axis))
    return jnp.concatenate([edge, body_part], axis)


def trilinear(brick, frac_x, frac_y, frac_z):
    depth = brick.ndim
    total = jnp.zeros_like(brick)
    for offset_x in (0, 1):
        moved_x = brick if offset_x == 0 else shift_up(brick, depth - 3)
        weight_x = 1.0 - frac_x if offset_x == 0 else frac_x
        for offset_y in (0, 1):
            moved = moved_x if offset_y == 0 else shift_up(moved_x, depth - 2)
            weight_y = 1.0 - frac_y if offset_y == 0 else frac_y
            along_z = (1.0 - frac_z) * moved + frac_z * shift_up(moved, depth - 1)
            total = total + weight_x * weight_y * along_z
    return total


def gradients(field):
    depth = field.ndim
    return jnp.stack(
        [
            0.5 * (shift_up(field, depth - 3 + offset) - shift_down(field, depth - 3 + offset))
            for offset in range(3)
        ]
    )


def smooth_z(field):
    depth = field.ndim
    return 0.25 * shift_down(field, depth - 1) + 0.5 * field + 0.25 * shift_up(field, depth - 1)


def predict(warped, grads, field):
    return warped + (grads[0] * field[0] + grads[1] * field[1]) + grads[2] * field[2]


def body(images, velocity, weights, template, owners, local_rows, tile_counts):
    spaces = lax.axis_size("space")
    groups = lax.axis_size("subj")
    subj_dev = images.shape[0]
    rows_dev = images.shape[1]
    plane = images.shape[2]
    depth_z = images.shape[3]
    cap = 2 * rows_dev // spaces
    subjects = subj_dev * groups
    position = jnp.arange(rows_dev, dtype=jnp.int32)[None, :]
    first = tile_counts // 2
    alive = (position < first) | (position >= rows_dev - (tile_counts - first))
    owner = owners[:, :, 0]
    hits = (owner[:, :, None] == jnp.arange(spaces, dtype=jnp.int32)[None, None, :]).astype(
        jnp.int32
    )
    hits = hits * alive.astype(jnp.int32)[:, :, None]
    before = jnp.cumsum(hits, axis=1) - hits
    place = jnp.sum(before * hits, axis=2)
    slot = jnp.where(alive, owner * cap + place, spaces * cap)
    request = jnp.zeros((subj_dev, spaces * cap), jnp.int32)
    request = request.at[jnp.arange(subj_dev)[:, None], slot].set(local_rows, mode="drop")
    request = request.reshape(subj_dev, spaces, cap)
    wanted = lax.all_to_all(request, "space", split_axis=1, concat_axis=1, tiled=True)
    returned = lax.all_to_all(
        jax.vmap(lambda image, index: image[index])(images, wanted),
        "space",
        split_axis=1,
        concat_axis=1,
        tiled=True,
    )
    returned = returned.reshape(subj_dev, spaces * cap, plane, depth_z)
    read_slot = jnp.minimum(slot, spaces * cap - 1)
    fetched = jax.vmap(lambda table, index: table[index])(returned, read_slot)
    live = alive.astype(jnp.float32)
    brick = fetched.astype(jnp.float32).reshape(subj_dev, rows_dev, BX, BY, depth_z)
    frac = weights.astype(jnp.float32).reshape(3, subj_dev, rows_dev, BX, BY, depth_z)
    warped = trilinear(brick, frac[0], frac[1], frac[2]) * live[:, :, None, None, None]
    grads = gradients(warped)
    whole = lax.all_gather(template, "subj", axis=1, tiled=True)
    current = whole.reshape(rows_dev, BX, BY, depth_z)
    field = velocity.reshape(3, subj_dev, rows_dev, BX, BY, depth_z)
    result = template
    for step in range(ITERS):
        predicted = predict(warped, grads, field)
        ratio = (predicted - current[None]) / (
            grads[0] * grads[0] + grads[1] * grads[1] + grads[2] * grads[2] + ridge
        )
        update = grads * ratio[None]
        padded = extended(update, (("space", 2),), 1)
        rowwise = 0.25 * padded[:, :, :-2] + 0.5 * update + 0.25 * padded[:, :, 2:]
        field = field - smooth_z(rowwise)
        local_sum = jnp.sum(predict(warped, grads, field), axis=0).reshape(rows_dev, plane, depth_z)
        share = lax.psum_scatter(local_sum, "subj", scatter_dimension=1, tiled=True) / subjects
        result = share
        if step + 1 < ITERS:
            current = (
                lax.all_gather(share.astype(jnp.bfloat16), "subj", axis=1, tiled=True)
                .astype(share.dtype)
                .reshape(rows_dev, BX, BY, depth_z)
            )
    return (field.reshape(3, subj_dev, rows_dev, plane, depth_z), result)


def solution(mesh):
    in_specs = (
        P("subj", "space", None, None),
        P(None, "subj", "space", None, None),
        P(None, "subj", "space", None, None),
        P("space", "subj", None),
        P("subj", "space", None),
        P("subj", "space"),
        P("subj", "space"),
    )
    out_specs = (P(None, "subj", "space", None, None), P("space", "subj", None))
    return jax.shard_map(body, mesh=mesh, in_specs=in_specs, out_specs=out_specs, check_vma=False)
```

profile of v0, /device:TPU:0, one launch (start us, length us, event | category | flops | bytes accessed | tf_op | source)
XLA Modules:
  0.0 179.5 jit_solution(12124676174121606328)
XLA Ops:
  7.2 0.8 reshape.243
  8.0 0.7 subtract_bitcast_fusion
  8.7 0.8 fusion.32
  9.5 0.1 reduce_window_sum.11
  9.6 0.9 fusion.31
  10.5 0.8 fusion.38
  11.4 6.4 %scatter_fusion = s32[2,128]{1,0:T(2,128)S(1)} fusion(s32[2,128]{1,0:T(2,128)S(1)} %broadcast_in_dim.10, s32[128]{0:T(128)S(1)} %reshape.241, s32[128]{0:T(128)S(1)} %reshape.243), kind=kCustom, calls=%fused_computation.2 | custom fusion | bytes 2560 | tf_op jit(solution)/shard_map/scatter | solution.py:93
  17.9 13.6 %all_to_all.10 = s32[2,8,16]{2,0,1:T(2,128)S(1)} all-to-all(s32[2,8,16]{2,0,1:T(2,128)S(1)} %copy.26), channel_id=1, replica_groups=mesh['subj'=4,'space'=8] {'space'}, dimensions={1} | all-to-all | bytes 2048 | tf_op jit(solution)/shard_map/all_to_all | solution.py:95
  31.6 1.2 gather_fusion
  32.8 1.1 copy.28
  34.0 4.3 %all-to-all-start.1 = ((bf16[2,8,16,16,128]{4,3,2,0,1:T(8,128)(2,1)}), bf16[2,8,16,16,128]{4,3,2,0,1:T(8,128)(2,1)}, u32[]{:S(2)}, u32[]{:S(2)}) async-start(bf16[2,8,16,16,128]{4,3,2,0,1:T(8,128)(2,1)} %copy.28), calls=%async_computation.1 | async-start | bytes 2097152 | tf_op jit(solution)/shard_map/all_to_all | solution.py:96
  38.4 7.2 %all_gather.6 = f32[64,16,128]{2,0,1:T(8,128)S(1)} all-gather(f32[64,4,128]{2,0,1:T(8,128)S(1)} %copy.30), channel_id=1, replica_groups=mesh['subj'=4,'space'=8] {'subj'}, dimensions={1}, use_global_device_ids=true | all-gather | bytes 655360 | tf_op jit(solution)/shard_map/all_gather | solution.py:111
  45.6 1.2 copy.31
  46.7 1.6 fusion.52
  48.3 1.1 copy-done.8
  49.4 1.7 fusion.51
  51.1 11.9 %all-to-all-done.1 = bf16[2,8,16,16,128]{4,3,2,0,1:T(8,128)(2,1)} async-done(((bf16[2,8,16,16,128]{4,3,2,0,1:T(8,128)(2,1)}), bf16[2,8,16,16,128]{4,3,2,0,1:T(8,128)(2,1)}, u32[]{:S(2)}, u32[]{:S(2)}) %all-to-all-start.1) | async-done | bytes 1048608 | tf_op jit(solution)/shard_map/all_to_all | solution.py:96
  63.0 1.4 copy.29
  64.4 0.9 gather_fusion.1
  65.4 0.1 slice.172
  65.5 0.3 slice.171
  65.8 0.3 slice.170
  66.1 0.2 pad_slice_fusion
  66.4 0.6 pad_slice_fusion.3
  67.0 1.0 pad_slice_fusion.1
  68.0 2.3 %fusion.12 = f32[2,64,4,4,128]{4,3,2,1,0:T(4,128)S(1)} fusion(f32[2,64,3,4,128]{4,3,2,1,0:T(4,128)S(1)} %slice.172, f32[2,64,4,4,128]{4,3,2,1,0:T(4,128)S(1)} %bitcast.108, f32[2,64,4,4,127]{4,3,2,1,0:T(4,128)S(1)} %get-tuple-element.41, f32[2,64,4,4,128]{4,3,2,1,0:T(4,128)S(1)} %bitcast.107, f32[2,64,4,4,128]{4,3,2,1,0:T(4,128)S(1)} %bitcast.106, ...), kind=kLoop, calls=%fused_computation.27 | loop fusion | flops 7340032 | bytes 11239936 | tf_op jit(solution)/shard_map/mul | solution.py:109
  70.4 0.3 fusion.55
  70.6 0.6 fusion.53
  71.3 0.4 fusion.54
  71.7 0.8 copy-done.14
  72.5 0.3 copy-done.15
  72.8 0.3 copy-done.16
  73.1 0.1 copy-done.19
  73.3 1.9 %subtract_divide_fusion.1 = (f32[2,64,4,4,128]{4,3,2,1,0:T(4,128)S(1)}, f32[2,64,4,4,128]{4,3,2,1,0:T(4,128)S(1)}, f32[2,64,4,4,128]{4,3,2,1,0:T(4,128)S(1)}, f32[1,2,64,4,4,128]{5,4,3,2,1,0:T(4,128)S(1)}) fusion(f32[2,64,4,4,128]{4,3,2,1,0:T(4,128)S(1)} %bitcast.104, f32[2,64,4,4,128]{4,3,2,1,0:T(4,128)S(1)} %fusion.12, ...), kind=kLoop, calls=%fused_computation.49 | loop fusion | flops 5242880 | bytes 14139392 | tf_op jit(solution)/shard_map/div | solution.py:117
  75.2 0.9 broadcast_multiply_fusion.1
  76.1 0.1 copy-done.11
  76.2 3.1 %collective-permute-start = (f32[3,2,1,4,4,128]{5,4,3,2,1,0:T(4,128)S(1)}, f32[3,2,1,4,4,128]{5,4,3,2,1,0:T(4,128)S(1)}, u32[]{:S(2)}, u32[]{:S(2)}) collective-permute-start(f32[3,2,1,4,4,128]{5,4,3,2,1,0:T(4,128)S(1)} %get-tuple-element.23), channel_id=1, source_target_pairs={{0,1},{1,2},{2,3},{3,4},{4,5},{5,6},{6,7},{8,9},{9,10},{10,11},{11... | collective-permute-start | bytes 147464 | tf_op jit(solution)/shard_map/ppermute | solution.py:19
  79.4 1.5 collective-permute-start.1
  80.9 0.3 collective-permute-done
  81.1 4.3 %collective-permute-done.1 = f32[3,2,1,4,4,128]{5,4,3,2,1,0:T(4,128)S(1)} collective-permute-done((f32[3,2,1,4,4,128]{5,4,3,2,1,0:T(4,128)S(1)}, f32[3,2,1,4,4,128]{5,4,3,2,1,0:T(4,128)S(1)}, u32[]{:S(2)}, u32[]{:S(2)}) %collective-permute-start.1) | collective-permute-done | bytes 49184 | tf_op jit(solution)/shard_map/ppermute | solution.py:22
  85.4 2.2 %fusion.5 = f32[3,2,64,4,4,128]{5,4,3,2,1,0:T(4,128)S(1)} fusion(f32[3,2,1,4,4,128]{5,4,3,2,1,0:T(4,128)S(1)} %collective-permute-done.1, f32[3,2,64,4,4,128]{5,4,3,2,1,0:T(4,128)S(1)} %broadcast_multiply_fusion.1, f32[3,2,1,4,4,128]{5,4,3,2,1,0:T(4,128)S(1)} %collective-permute-done), kind=kLoop, calls=%fused_computation.11 | loop fusion | flops 5505024 | bytes 6389760 | tf_op jit(solution)/shard_map/add | solution.py:122
  87.6 2.1 %fusion.49 = (f32[3,2,64,4,4,127]{5,4,3,2,1,0:T(4,128)S(1)}, f32[3,2,64,4,4,127]{5,4,3,2,1,0:T(4,128)S(1)}) fusion(f32[3,2,64,4,4,128]{5,4,3,2,1,0:T(4,128)S(1)} %fusion.5), kind=kLoop, calls=%fused_computation.97 | loop fusion | bytes 12484608 | tf_op jit(solution)/shard_map/slice | solution.py:34
  89.8 4.2 %add_subtract_fusion.1 = f32[3,2,64,4,4,128]{5,4,3,2,1,0:T(4,128)S(1)} fusion(f32[3,2,64,4,4,128]{5,4,3,2,1,0:T(4,128)S(1)} %bitcast.101, f32[3,2,64,4,4,127]{5,4,3,2,1,0:T(4,128)S(1)} %get-tuple-element.22, f32[3,2,64,4,4,127]{5,4,3,2,1,0:T(4,128)S(1)} %get-tuple-element.21, f32[3,2,1,4,4,128]{5,4,3,2,1,0:T(4,128)S(1)} %collective-permute-done.1, ...), kind=kLoop, calls=%fused_computation.17 | loop fusion | flops 10223616 | bytes 15777792 | tf_op jit(solution)/shard_map/sub | solution.py:123
  94.0 2.5 %fusion.45 = (f32[64,4,4,128]{3,2,1,0:T(4,128)S(1)}, f32[2,64,4,4,128]{4,3,2,1,0:T(4,128)}) fusion(f32[2,64,4,4,128]{4,3,2,1,0:T(4,128)S(1)} %get-tuple-element.12, f32[3,2,64,4,4,128]{5,4,3,2,1,0:T(4,128)S(1)} %add_subtract_fusion.1, f32[2,64,4,4,128]{4,3,2,1,0:T(4,128)S(1)} %fusion.12, f32[2,64,4,4,128]{4,3,2,1,0:T(4,128)S(1)} %get-tuple-element.11, ...), kind=kLoop, calls=%fused_computation.94 | loop fusion | flops 2228224 | bytes 9437184 | tf_op jit(solution)/shard_map/reduce_sum | solution.py:124
  96.5 1.0 copy.32
  97.6 20.5 %reduce-scatter.3.cloned.1.call-done = f32[64,4,128]{2,0,1:T(8,128)} async-done(((f32[64,16,128]{2,0,1:T(8,128)}), f32[64,4,128]{2,0,1:T(8,128)}) %reduce-scatter.3.cloned.1.call-update) | async-done | bytes 131088 | tf_op jit(solution)/shard_map/reduce_scatter | solution.py:125
  118.1 0.9 multiply_convert_fusion
  119.0 5.8 %all_gather.7 = bf16[64,16,128]{2,0,1:T(8,128)(2,1)S(1)} all-gather(bf16[64,4,128]{2,0,1:T(8,128)(2,1)S(1)} %multiply_convert_fusion), channel_id=1, replica_groups=mesh['subj'=4,'space'=8] {'subj'}, dimensions={1}, use_global_device_ids=true | all-gather | bytes 327680 | tf_op jit(solution)/shard_map/all_gather | solution.py:129
  124.8 0.2 copy.33
  125.0 2.6 %subtract_divide_fusion = f32[2,64,4,4,128]{4,3,2,1,0:T(4,128)S(1)} fusion(f32[2,64,4,4,128]{4,3,2,1,0:T(4,128)} %get-tuple-element.9, f32[64,4,4,128]{3,2,1,0:T(4,128)S(1)} %copy.33, f32[2,64,4,4,128]{4,3,2,1,0:T(4,128)} %copy-done.2, f32[2,64,4,4,128]{4,3,2,1,0:T(4,128)S(1)} %get-tuple-element.11, f32[2,64,3,4,128]{4,3,2,1,0:T(4,128)} %copy-done.6, ...), kind=kLoop, calls=%fused_computation.47 | loop fusion | flops 2621440 | bytes 6291456 | tf_op jit(solution)/shard_map/div | solution.py:117
  127.7 0.9 broadcast_multiply_fusion
  128.6 3.4 %collective-permute-start.2 = (f32[3,2,1,4,4,128]{5,4,3,2,1,0:T(4,128)S(1)}, f32[3,2,1,4,4,128]{5,4,3,2,1,0:T(4,128)S(1)}, u32[]{:S(2)}, u32[]{:S(2)}) collective-permute-start(f32[3,2,1,4,4,128]{5,4,3,2,1,0:T(4,128)S(1)} %get-tuple-element.19), channel_id=1, source_target_pairs={{0,1},{1,2},{2,3},{3,4},{4,5},{5,6},{6,7},{8,9},{9,10},{10,11},{11... | collective-permute-start | bytes 147464 | tf_op jit(solution)/shard_map/ppermute | solution.py:19
  132.0 1.5 collective-permute-start.3
  133.5 0.2 collective-permute-done.2
  133.7 4.3 %collective-permute-done.3 = f32[3,2,1,4,4,128]{5,4,3,2,1,0:T(4,128)S(1)} collective-permute-done((f32[3,2,1,4,4,128]{5,4,3,2,1,0:T(4,128)S(1)}, f32[3,2,1,4,4,128]{5,4,3,2,1,0:T(4,128)S(1)}, u32[]{:S(2)}, u32[]{:S(2)}) %collective-permute-start.3) | collective-permute-done | bytes 49184 | tf_op jit(solution)/shard_map/ppermute | solution.py:22
  138.0 2.2 %fusion.1 = f32[3,2,64,4,4,128]{5,4,3,2,1,0:T(4,128)S(1)} fusion(f32[3,2,1,4,4,128]{5,4,3,2,1,0:T(4,128)S(1)} %collective-permute-done.3, f32[3,2,64,4,4,128]{5,4,3,2,1,0:T(4,128)S(1)} %broadcast_multiply_fusion, f32[3,2,1,4,4,128]{5,4,3,2,1,0:T(4,128)S(1)} %collective-permute-done.2), kind=kLoop, calls=%fused_computation.5 | loop fusion | flops 5505024 | bytes 6389760 | tf_op jit(solution)/shard_map/add | solution.py:122
  140.2 2.1 %fusion.47 = (f32[3,2,64,4,4,127]{5,4,3,2,1,0:T(4,128)S(1)}, f32[3,2,64,4,4,127]{5,4,3,2,1,0:T(4,128)S(1)}) fusion(f32[3,2,64,4,4,128]{5,4,3,2,1,0:T(4,128)S(1)} %fusion.1), kind=kLoop, calls=%fused_computation.95 | loop fusion | bytes 12484608 | tf_op jit(solution)/shard_map/slice | solution.py:34
  142.4 4.2 %add_subtract_fusion = f32[3,2,64,4,4,128]{5,4,3,2,1,0:T(4,128)S(1)} fusion(f32[3,2,64,4,4,128]{5,4,3,2,1,0:T(4,128)S(1)} %copy-done.5, f32[3,2,64,4,4,127]{5,4,3,2,1,0:T(4,128)S(1)} %get-tuple-element.18, f32[3,2,64,4,4,127]{5,4,3,2,1,0:T(4,128)S(1)} %get-tuple-element.17, f32[3,2,1,4,4,128]{5,4,3,2,1,0:T(4,128)S(1)} %collective-permute-done.3, ...), kind=kLoop, calls=%fused_computation.16 | loop fusion | flops 10223616 | bytes 15777792 | tf_op jit(solution)/shard_map/sub | solution.py:123
  146.6 1.5 fusion.15
  148.1 0.1 copy-done.10
  148.2 1.0 copy.34
  149.2 21.8 %reduce-scatter.5.cloned.1.call-done = f32[64,4,128]{2,0,1:T(8,128)} async-done(((f32[64,16,128]{2,0,1:T(8,128)}), f32[64,4,128]{2,0,1:T(8,128)}) %reduce-scatter.5.cloned.1.call-update) | async-done | bytes 131088 | tf_op jit(solution)/shard_map/reduce_scatter | solution.py:125
  171.0 0.9 broadcast_multiply_fusion.2
  172.0 0.7 copy.35
  (52 shorter events, 0.7 us)
Async XLA Ops:
  7.2 24.4 %copy-start = (bf16[2,64,16,128]{3,2,1,0:T(8,128)(2,1)S(1)}, bf16[2,64,16,128]{3,2,1,0:T(8,128)(2,1)}, u32[]{:S(2)}) copy-start(bf16[2,64,16,128]{3,2,1,0:T(8,128)(2,1)} %param.7) | copy-start | bytes 1572868
  31.6 6.8 %copy-start.20 = (f32[64,4,128]{2,1,0:T(4,128)S(1)}, f32[64,4,128]{2,1,0:T(4,128)}, u32[]{:S(2)}) copy-start(f32[64,4,128]{2,1,0:T(4,128)} %param.10) | copy-start | bytes 393220
  32.8 13.9 %copy-start.13 = (bf16[3,2,64,16,128]{4,3,2,1,0:T(8,128)(2,1)S(1)}, bf16[3,2,64,16,128]{4,3,2,1,0:T(8,128)(2,1)}, u32[]{:S(2)}) copy-start(bf16[3,2,64,16,128]{4,3,2,1,0:T(8,128)(2,1)} %param.9) | copy-start | bytes 4718596
  34.0 29.1 %all-to-all-start.1 = ((bf16[2,8,16,16,128]{4,3,2,0,1:T(8,128)(2,1)}), bf16[2,8,16,16,128]{4,3,2,0,1:T(8,128)(2,1)}, u32[]{:S(2)}, u32[]{:S(2)}) async-start(bf16[2,8,16,16,128]{4,3,2,0,1:T(8,128)(2,1)} %copy.28), calls=%async_computation.1 | async-start | bytes 2097152 | tf_op jit(solution)/shard_map/all_to_all | solution.py:96
  38.2 79.9 %reduce-scatter.3.cloned.1.call-start = ((), (), s32[]{:S(2)}) async-start(), calls=%async_computation.4 | async-start | bytes 655360 | tf_op jit(solution)/shard_map/reduce_scatter | solution.py:125
  46.7 2.6 %copy-start.8 = (f32[3,2,64,16,128]{4,3,2,1,0:T(8,128)S(1)}, f32[3,2,64,16,128]{4,3,2,1,0:T(8,128)}, u32[]{:S(2)}) copy-start(f32[3,2,64,16,128]{4,3,2,1,0:T(8,128)} %param.8) | copy-start | bytes 9437188
  66.3 1.6 copy-start.17
  66.4 1.6 copy-start.18
  70.6 23.3 %copy-start.6 = (f32[2,64,3,4,128]{4,3,2,1,0:T(4,128)}, f32[2,64,3,4,128]{4,3,2,1,0:T(4,128)S(1)}, u32[]{:S(2)}) copy-start(f32[2,64,3,4,128]{4,3,2,1,0:T(4,128)S(1)} %get-tuple-element.37) | copy-start | bytes 2359300
  71.3 1.2 copy-start.14
  71.3 1.5 copy-start.15
  71.3 1.8 %copy-start.16 = (f32[1,2,64,16,128]{4,3,2,1,0:T(8,128)S(1)}, f32[1,2,64,16,128]{4,3,2,1,0:T(8,128)}, u32[]{:S(2)}) copy-start(f32[1,2,64,16,128]{4,3,2,1,0:T(8,128)} %get-tuple-element.27) | copy-start | bytes 3145732
  71.3 2.0 %copy-start.19 = (f32[64,4,4,128]{3,2,1,0:T(4,128)S(1)}, f32[64,4,4,128]{3,2,1,0:T(4,128)}, u32[]{:S(2)}) copy-start(f32[64,4,4,128]{3,2,1,0:T(4,128)} %copy.31) | copy-start | bytes 1572868
  75.2 1.0 copy-start.11
  75.2 18.7 %copy-start.2 = (f32[2,64,4,4,128]{4,3,2,1,0:T(4,128)}, f32[2,64,4,4,128]{4,3,2,1,0:T(4,128)S(1)}, u32[]{:S(2)}) copy-start(f32[2,64,4,4,128]{4,3,2,1,0:T(4,128)S(1)} %get-tuple-element.12) | copy-start | bytes 3145732
  76.2 4.9 %collective-permute-start = (f32[3,2,1,4,4,128]{5,4,3,2,1,0:T(4,128)S(1)}, f32[3,2,1,4,4,128]{5,4,3,2,1,0:T(4,128)S(1)}, u32[]{:S(2)}, u32[]{:S(2)}) collective-permute-start(f32[3,2,1,4,4,128]{5,4,3,2,1,0:T(4,128)S(1)} %get-tuple-element.23), channel_id=1, source_target_pairs={{0,1},{1,2},{2,3},{3,4},{4,5},{5,6},{6,7},{8,9},{9,10},{10,11},{11... | collective-permute-start | bytes 147464 | tf_op jit(solution)/shard_map/ppermute | solution.py:19
  79.4 6.0 %collective-permute-start.1 = (f32[3,2,1,4,4,128]{5,4,3,2,1,0:T(4,128)S(1)}, f32[3,2,1,4,4,128]{5,4,3,2,1,0:T(4,128)S(1)}, u32[]{:S(2)}, u32[]{:S(2)}) collective-permute-start(f32[3,2,1,4,4,128]{5,4,3,2,1,0:T(4,128)S(1)} %get-tuple-element.24), channel_id=1, source_target_pairs={{1,0},{2,1},{3,2},{4,3},{5,4},{6,5},{7,6},{9,8},{10,9},{11,10},{12... | collective-permute-start | bytes 147464 | tf_op jit(solution)/shard_map/ppermute | solution.py:22
  87.6 2.2 %copy-start.9 = (f32[3,2,64,16,128]{4,3,2,1,0:T(8,128)S(1)}, f32[3,2,64,16,128]{4,3,2,1,0:T(8,128)}, u32[]{:S(2)}) copy-start(f32[3,2,64,16,128]{4,3,2,1,0:T(8,128)} %param.8) | copy-start | bytes 9437188
  94.0 2.5 %copy-start.4 = (f32[3,2,64,4,4,128]{5,4,3,2,1,0:T(4,128)}, f32[3,2,64,4,4,128]{5,4,3,2,1,0:T(4,128)S(1)}, u32[]{:S(2)}) copy-start(f32[3,2,64,4,4,128]{5,4,3,2,1,0:T(4,128)S(1)} %add_subtract_fusion.1) | copy-start | bytes 9437188
  97.5 73.5 %reduce-scatter.5.cloned.1.call-start = ((), (), s32[]{:S(2)}) async-start(), calls=%async_computation.5 | async-start | bytes 655360 | tf_op jit(solution)/shard_map/reduce_scatter | solution.py:125
  125.0 2.7 %copy-start.3 = (f32[2,64,4,4,128]{4,3,2,1,0:T(4,128)S(1)}, f32[2,64,4,4,128]{4,3,2,1,0:T(4,128)}, u32[]{:S(2)}) copy-start(f32[2,64,4,4,128]{4,3,2,1,0:T(4,128)} %copy-done.2) | copy-start | bytes 3145732
  125.0 2.7 %copy-start.12 = (f32[1,2,64,4,4,128]{5,4,3,2,1,0:T(4,128)S(1)}, f32[1,2,64,4,4,128]{5,4,3,2,1,0:T(4,128)}, u32[]{:S(2)}) copy-start(f32[1,2,64,4,4,128]{5,4,3,2,1,0:T(4,128)} %copy-done.11) | copy-start | bytes 3145732
  128.6 5.1 %collective-permute-start.2 = (f32[3,2,1,4,4,128]{5,4,3,2,1,0:T(4,128)S(1)}, f32[3,2,1,4,4,128]{5,4,3,2,1,0:T(4,128)S(1)}, u32[]{:S(2)}, u32[]{:S(2)}) collective-permute-start(f32[3,2,1,4,4,128]{5,4,3,2,1,0:T(4,128)S(1)} %get-tuple-element.19), channel_id=1, source_target_pairs={{0,1},{1,2},{2,3},{3,4},{4,5},{5,6},{6,7},{8,9},{9,10},{10,11},{11... | collective-permute-start | bytes 147464 | tf_op jit(solution)/shard_map/ppermute | solution.py:19
  132.0 6.0 %collective-permute-start.3 = (f32[3,2,1,4,4,128]{5,4,3,2,1,0:T(4,128)S(1)}, f32[3,2,1,4,4,128]{5,4,3,2,1,0:T(4,128)S(1)}, u32[]{:S(2)}, u32[]{:S(2)}) collective-permute-start(f32[3,2,1,4,4,128]{5,4,3,2,1,0:T(4,128)S(1)} %get-tuple-element.20), channel_id=1, source_target_pairs={{1,0},{2,1},{3,2},{4,3},{5,4},{6,5},{7,6},{9,8},{10,9},{11,10},{12... | collective-permute-start | bytes 147464 | tf_op jit(solution)/shard_map/ppermute | solution.py:22
  140.2 2.2 %copy-start.5 = (f32[3,2,64,4,4,128]{5,4,3,2,1,0:T(4,128)S(1)}, f32[3,2,64,4,4,128]{5,4,3,2,1,0:T(4,128)}, u32[]{:S(2)}) copy-start(f32[3,2,64,4,4,128]{5,4,3,2,1,0:T(4,128)} %copy-done.4) | copy-start | bytes 9437188
  142.4 4.2 %copy-start.7 = (f32[2,64,3,4,128]{4,3,2,1,0:T(4,128)S(1)}, f32[2,64,3,4,128]{4,3,2,1,0:T(4,128)}, u32[]{:S(2)}) copy-start(f32[2,64,3,4,128]{4,3,2,1,0:T(4,128)} %copy-done.6) | copy-start | bytes 2359300
  146.6 1.7 copy-start.10
  146.6 26.1 %copy-start.1 = (bf16[2,64,16,128]{3,2,1,0:T(8,128)(2,1)S(1)}, bf16[2,64,16,128]{3,2,1,0:T(8,128)(2,1)}, u32[]{:S(2)}) copy-start(bf16[2,64,16,128]{3,2,1,0:T(8,128)(2,1)} %param.7) | copy-start | bytes 1572868
Sparse Core Ops, SparseCore 0:
  97.6 20.4 reduce-scatter.2
  149.4 21.6 reduce-scatter.4
where the time goes:
time: 180 us
  waiting for transfers between devices  63.3 us (35%)
  local copies, waits for them, and re-layouts  30.8 us (17%)
  other arithmetic  30.6 us (17%)
  blocking collectives  26.5 us (15%)
  between operations  14.5 us (8%)
  starting transfers between devices  13.8 us (8%)
    reduce_scatter x2, waiting for transfers between devices, body(): lax.psum_scatter(local_sum, 'subj', scatter_dimension=1, tiled=True)  42.3 us
    all_to_all x1, blocking collectives, body(): lax.all_to_all(request, 'space', split_axis=1, concat_axis=1, tiled=True)  13.6 us
    all_to_all x1, waiting for transfers between devices, body(): lax.all_to_all(jax.vmap(lambda image, index: image[index])(images, wanted...  11.9 us
    ppermute x2, waiting for transfers between devices, extended(): lax.ppermute(lax.slice_in_dim(block, 0, width, axis=dim), axis, backward)  8.5 us
    sub x2, other arithmetic, body(): field = field - smooth_z(rowwise)  8.33 us
    all_gather x1, blocking collectives, body(): whole = lax.all_gather(template, 'subj', axis=1, tiled=True)  7.17 us
    ppermute x2, starting transfers between devices, extended(): lax.ppermute(lax.slice_in_dim(block, block.shape[dim] - width, None, axis...  6.52 us
    scatter x1, local copies, waits for them, and re-layouts, body(): request.at[jnp.arange(subj_dev)[:, None], slot].set(local_rows, mode='drop')  6.43 us
  transfers between devices with their start and end apart: 7, of which 7 were waited for; matrix products, arithmetic and copies ran while one was open for 3% of the time, Pallas kernels for 0%

commit v1 on v0

v1 whole, which is shorter than its diff:
```python
import functools

import jax
import jax.numpy as jnp
from jax import lax
from jax.experimental import pallas as pl
from jax.experimental.pallas import tpu as pltpu
from jax.sharding import PartitionSpec as P

BY = 4
ITERS = 2
RIDGE = 0.25
LANES = 128
BLOCK = 16
LIMIT = 48 * 1024 * 1024


def params():
    return pltpu.CompilerParams(vmem_limit_bytes=LIMIT)


VMEM = pl.BlockSpec(memory_space=pltpu.VMEM)
SMEM = pl.BlockSpec(memory_space=pltpu.SMEM)
ANY = pl.BlockSpec(memory_space=pl.ANY)


def plan_kernel(cap, counts_ref, owners_ref, rows_ref, request_ref, slots_ref):
    subj_dev, rows = rows_ref.shape
    spaces = request_ref.shape[0]
    t = lax.broadcasted_iota(jnp.int32, (rows, rows), 0)
    u = lax.broadcasted_iota(jnp.int32, (rows, rows), 1)
    eye = t == u
    lane = lax.broadcasted_iota(jnp.int32, (rows, LANES), 1)
    sub = lax.broadcasted_iota(jnp.int32, (spaces, LANES), 0)
    zero = jnp.zeros((rows, rows), jnp.int32)
    request = jnp.zeros((spaces, LANES), jnp.int32)
    earlier_subjects = []
    for s in range(subj_dev):
        count = counts_ref[s, 0]
        first = lax.shift_right_logical(count, 1)
        owner_t = jnp.broadcast_to(owners_ref[s], (rows, rows))
        owner_u = jnp.broadcast_to(
            jnp.sum(jnp.where(eye, owner_t, zero), axis=0, keepdims=True), (rows, rows)
        )
        row_u = jnp.broadcast_to(rows_ref[s : s + 1, :], (rows, rows))
        row_t = jnp.broadcast_to(
            jnp.sum(jnp.where(eye, row_u, zero), axis=1, keepdims=True), (rows, rows)
        )
        last = rows - (count - first)
        alive_t = (t < first) | (t >= last)
        alive_u = (u < first) | (u >= last)
        same_owner = owner_t == owner_u
        same = same_owner & (row_t == row_u)
        dup_u = jnp.sum(jnp.where(same & alive_t & (t < u), 1, 0), axis=0, keepdims=True)
        dup_t = jnp.sum(jnp.where(same & alive_u & (u < t), 1, 0), axis=1, keepdims=True)
        first_u = alive_u & jnp.broadcast_to(dup_u == 0, (rows, rows))
        first_t = alive_t & jnp.broadcast_to(dup_t == 0, (rows, rows))
        place = jnp.sum(
            jnp.where(same_owner & first_u & (u < t), 1, 0), axis=1, keepdims=True
        )
        for owner_v, first_v in earlier_subjects:
            place = place + jnp.sum(
                jnp.where((owner_t == owner_v) & first_v, 1, 0), axis=1, keepdims=True
            )
        earlier_subjects.append((owner_u, first_u))
        slot_t = owner_t * cap + place
        slots_ref[s : s + 1, :] = jnp.sum(
            jnp.where(same & first_t & alive_u, slot_t, zero), axis=0, keepdims=True
        )
        wide_first = jnp.broadcast_to(first_t[:, :1], (rows, LANES))
        wide_owner = jnp.broadcast_to(owner_t[:, :1], (rows, LANES))
        wide_place = jnp.broadcast_to(place, (rows, LANES))
        wide_row = jnp.broadcast_to(row_t[:, :1], (rows, LANES)) + s * rows
        hit = jnp.where(wide_first & (wide_place == lane), wide_row, 0)
        for o in range(spaces):
            line = jnp.sum(jnp.where(wide_owner == o, hit, 0), axis=0, keepdims=True)
            request = request + jnp.where(sub == o, line, 0)
    request_ref[...] = request


def plan(counts, owners, local_rows, cap, spaces):
    subj_dev, rows = local_rows.shape
    return pl.pallas_call(
        functools.partial(plan_kernel, cap),
        out_shape=(
            jax.ShapeDtypeStruct((spaces, LANES), jnp.int32),
            jax.ShapeDtypeStruct((subj_dev, rows), jnp.int32),
        ),
        in_specs=[SMEM, VMEM, VMEM],
        out_specs=(VMEM, VMEM),
        compiler_params=params(),
        name="plan",
    )(counts, owners, local_rows)


def pick_kernel(me_ref, wanted_ref, images_ref, *outs):
    me = me_ref[0]
    for k, out in enumerate(outs):
        target = lax.bitwise_xor(me, k)
        for c in range(out.shape[0]):
            out[c] = images_ref[wanted_ref[target, c]]


def pick(me, wanted, images, cap):
    spaces = wanted.shape[0]
    one = jax.ShapeDtypeStruct((cap,) + images.shape[1:], images.dtype)
    return pl.pallas_call(
        pick_kernel,
        out_shape=[one] * spaces,
        in_specs=[SMEM, SMEM, VMEM],
        out_specs=[VMEM] * spaces,
        compiler_params=params(),
        name="pick",
    )(me, wanted, images)


def up_x(v):
    return pltpu.roll(v, v.shape[0] - BY, 0)


def up_y(v):
    return pltpu.roll(v, v.shape[0] - 1, 0)


def up_z(v):
    return pltpu.roll(v, v.shape[1] - 1, 1)


def down_x(v):
    return pltpu.roll(v, BY, 0)


def down_y(v):
    return pltpu.roll(v, 1, 0)


def down_z(v):
    return pltpu.roll(v, 1, 1)


def edges(shape, value):
    p = lax.broadcasted_iota(jnp.int32, shape, 0)
    z = lax.broadcasted_iota(jnp.int32, shape, 1)
    y = lax.bitwise_and(p, BY - 1)
    conditions = (
        p < shape[0] - BY,
        p >= BY,
        y < BY - 1,
        y > 0,
        z < shape[1] - 1,
        z > 0,
    )
    return [jnp.where(c, value, 0.0).astype(jnp.float32) for c in conditions]


def warp_tile(brick, frac_x, frac_y, frac_z, masks, live):
    frac_x, frac_y, frac_z = (f.astype(jnp.float32) for f in (frac_x, frac_y, frac_z))
    high_x, high_y, high_z = frac_x * masks[0], frac_y * masks[2], frac_z * masks[4]
    low_x, low_y, low_z = 1.0 - frac_x, 1.0 - frac_y, 1.0 - frac_z
    low_x, high_x = low_x * live, high_x * live

    def along_z(v):
        return low_z * v + high_z * up_z(v)

    def along_y(v):
        return low_y * along_z(v) + high_y * along_z(up_y(v))

    return low_x * along_y(brick) + high_x * along_y(up_x(brick))


def warp_kernel(spaces, me_ref, counts_ref, slots_ref, *refs):
    parts = refs[:spaces]
    weights_ref, warped_ref, low_ref, high_ref, table, sems = refs[spaces:]
    _, subj_dev, block, plane, depth = weights_ref.shape
    cap = table.shape[0] // spaces
    step, steps = pl.program_id(0), pl.num_programs(0)
    me = me_ref[0]

    @pl.when(step == 0)
    def _():
        copies = [
            pltpu.make_async_copy(part, table.at[pl.ds(k * cap, cap)], sems.at[k])
            for k, part in enumerate(parts)
        ]
        for copy in copies:
            copy.start()
        for copy in copies:
            copy.wait()

    masks = edges((plane, depth), 1.0)

    def tile(r, carry):
        t = step * block + r
        for s in range(subj_dev):
            count = counts_ref[s, 0]
            first = lax.shift_right_logical(count, 1)
            rows = steps * block
            alive = (t < first) | (t >= rows - (count - first))
            live = jnp.where(alive, 1.0, 0.0).astype(jnp.float32)
            slot = lax.bitwise_xor(slots_ref[s, t], me * cap)
            brick = table[slot].astype(jnp.float32)
            warped_ref[s, r] = warp_tile(
                brick, weights_ref[0, s, r], weights_ref[1, s, r], weights_ref[2, s, r], masks, live
            )
        return carry

    lax.fori_loop(0, block, tile, 0, unroll=4)

    @pl.when(step == 0)
    def _():
        low_ref[...] = warped_ref[:, :2]

    @pl.when(step == steps - 1)
    def _():
        high_ref[...] = warped_ref[:, block - 2 :]


def warp(me, counts, slots, parts, weights):
    _, subj_dev, rows, plane, depth = weights.shape
    spaces = len(parts)
    cap = parts[0].shape[0]
    edge = jax.ShapeDtypeStruct((subj_dev, 2, plane, depth), jnp.float32)
    edge_spec = pl.BlockSpec((subj_dev, 2, plane, depth), lambda i: (0, 0, 0, 0))
    return pl.pallas_call(
        functools.partial(warp_kernel, spaces),
        grid=(rows // BLOCK,),
        out_shape=(jax.ShapeDtypeStruct((subj_dev, rows, plane, depth), jnp.float32), edge, edge),
        in_specs=[SMEM] * 3
        + [ANY] * spaces
        + [pl.BlockSpec((3, subj_dev, BLOCK, plane, depth), lambda i: (0, 0, i, 0, 0))],
        out_specs=(
            pl.BlockSpec((subj_dev, BLOCK, plane, depth), lambda i: (0, i, 0, 0)),
            edge_spec,
            edge_spec,
        ),
        scratch_shapes=[
            pltpu.VMEM((spaces * cap, plane, depth), jnp.bfloat16),
            pltpu.SemaphoreType.DMA((spaces,)),
        ],
        compiler_params=params(),
        name="warp",
    )(me, counts, slots, *parts, weights)


def slopes(w, halves):
    return (
        up_x(w) * halves[0] - down_x(w) * halves[1],
        up_y(w) * halves[2] - down_y(w) * halves[3],
        up_z(w) * halves[4] - down_z(w) * halves[5],
    )


def predict(w, g, f):
    return w + (g[0] * f[0] + g[1] * f[1]) + g[2] * f[2]


def update_of(w, f, current, halves):
    g = slopes(w, halves)
    ratio = (predict(w, g, f) - current) / (g[0] * g[0] + g[1] * g[1] + g[2] * g[2] + RIDGE)
    return [g[c] * ratio for c in range(3)]


def smooth(before, here, after, halves):
    rowwise = 0.25 * before + 0.5 * here + 0.25 * after
    return (
        (0.5 * halves[5]) * down_z(rowwise)
        + 0.5 * rowwise
        + (0.5 * halves[4]) * up_z(rowwise)
    )


def update_kernel(warped_ref, field_ref, current_ref, update_ref):
    subj_dev, block, plane, depth = warped_ref.shape
    halves = edges((plane, depth), 0.5)

    def tile(r, carry):
        current = current_ref[r]
        for s in range(subj_dev):
            f = [field_ref[c, s, r] for c in range(3)]
            u = update_of(warped_ref[s, r], f, current, halves)
            for c in range(3):
                update_ref[c, s, r] = u[c]
        return carry

    lax.fori_loop(0, block, tile, 0, unroll=4)


def update(warped, field, current):
    _, subj_dev, rows, plane, depth = field.shape
    five = pl.BlockSpec((3, subj_dev, BLOCK, plane, depth), lambda i: (0, 0, i, 0, 0))
    return pl.pallas_call(
        update_kernel,
        grid=(rows // BLOCK,),
        out_shape=jax.ShapeDtypeStruct(field.shape, jnp.float32),
        in_specs=[
            pl.BlockSpec((subj_dev, BLOCK, plane, depth), lambda i: (0, i, 0, 0)),
            five,
            pl.BlockSpec((BLOCK, plane, depth), lambda i: (i, 0, 0)),
        ],
        out_specs=five,
        compiler_params=params(),
        name="update",
    )(warped, field, current)


def store_sum(keep_ref, send_ref, row, total, core):
    half = total.shape[0] // 2
    low, high = total[:half], total[half:]
    keep_ref[row] = jnp.where(core == 0, low, high)
    send_ref[row] = jnp.where(core == 0, high, low)


def move_kernel(
    core_ref,
    update_ref,
    before_ref,
    after_ref,
    warped_ref,
    field_ref,
    halo_warped_ref,
    halo_field_ref,
    halo_current_ref,
    moved_ref,
    halo_moved_ref,
    keep_ref,
    send_ref,
    halo_update,
):
    subj_dev, block, plane, depth = warped_ref.shape
    step, steps = pl.program_id(0), pl.num_programs(0)
    core = core_ref[0]
    halves = edges((plane, depth), 0.5)

    @pl.when(step == 0)
    def _():
        for s in range(subj_dev):
            for h in range(4):
                f = [halo_field_ref[c, s, h] for c in range(3)]
                u = update_of(halo_warped_ref[s, h], f, halo_current_ref[h], halves)
                for c in range(3):
                    halo_update[c, s, h] = u[c]

    def halo_row(h, out, row, neighbours):
        total = None
        for s in range(subj_dev):
            w = halo_warped_ref[s, h]
            g = slopes(w, halves)
            f = []
            for c in range(3):
                before, here, after = neighbours(c, s)
                f.append(halo_field_ref[c, s, h] - smooth(before, here, after, halves))
                halo_moved_ref[c, s, out] = f[c]
            p = predict(w, g, f)
            total = p if total is None else total + p
        store_sum(keep_ref, send_ref, row, total, core)

    @pl.when(step == 0)
    def _():
        halo_row(
            1,
            0,
            0,
            lambda c, s: (halo_update[c, s, 0], halo_update[c, s, 1], update_ref[c, s, 0]),
        )

    @pl.when(step == steps - 1)
    def _():
        halo_row(
            2,
            1,
            steps * block + 1,
            lambda c, s: (update_ref[c, s, block - 1], halo_update[c, s, 2], halo_update[c, s, 3]),
        )

    def row_of(r, before_of, after_of):
        total = None
        for s in range(subj_dev):
            w = warped_ref[s, r]
            g = slopes(w, halves)
            f = []
            for c in range(3):
                delta = smooth(before_of(c, s), update_ref[c, s, r], after_of(c, s), halves)
                f.append(field_ref[c, s, r] - delta)
                moved_ref[c, s, r] = f[c]
            p = predict(w, g, f)
            total = p if total is None else total + p
        store_sum(keep_ref, send_ref, step * block + r + 1, total, core)

    row_of(
        0,
        lambda c, s: jnp.where(step == 0, halo_update[c, s, 1], before_ref[c, s, 0]),
        lambda c, s: update_ref[c, s, 1],
    )

    def tile(r, carry):
        row_of(
            r, lambda c, s: update_ref[c, s, r - 1], lambda c, s: update_ref[c, s, r + 1]
        )
        return carry

    lax.fori_loop(1, block - 1, tile, 0, unroll=2)
    row_of(
        block - 1,
        lambda c, s: update_ref[c, s, block - 2],
        lambda c, s: jnp.where(step == steps - 1, halo_update[c, s, 2], after_ref[c, s, 0]),
    )


def move(core, updates, warped, field, halo_warped, halo_field, halo_current):
    _, subj_dev, rows, plane, depth = field.shape
    five = pl.BlockSpec((3, subj_dev, BLOCK, plane, depth), lambda i: (0, 0, i, 0, 0))
    line = (3, subj_dev, 1, plane, depth)
    halo_moved = jax.ShapeDtypeStruct((3, subj_dev, 2, plane, depth), jnp.float32)
    sums = jax.ShapeDtypeStruct((rows + 2, plane // 2, depth), jnp.float32)
    return pl.pallas_call(
        move_kernel,
        grid=(rows // BLOCK,),
        out_shape=(
            jax.ShapeDtypeStruct(field.shape, jnp.float32),
            halo_moved,
            sums,
            sums,
        ),
        in_specs=[
            SMEM,
            five,
            pl.BlockSpec(line, lambda i: (0, 0, jnp.maximum(i * BLOCK - 1, 0), 0, 0)),
            pl.BlockSpec(line, lambda i: (0, 0, jnp.minimum(i * BLOCK + BLOCK, rows - 1), 0, 0)),
            pl.BlockSpec((subj_dev, BLOCK, plane, depth), lambda i: (0, i, 0, 0)),
            five,
            VMEM,
            VMEM,
            VMEM,
        ],
        out_specs=(
            five,
            pl.BlockSpec(halo_moved.shape, lambda i: (0, 0, 0, 0, 0)),
            pl.BlockSpec(sums.shape, lambda i: (0, 0, 0)),
            pl.BlockSpec(sums.shape, lambda i: (0, 0, 0)),
        ),
        scratch_shapes=[pltpu.VMEM((3, subj_dev, 4, plane, depth), jnp.float32)],
        compiler_params=params(),
        name="move",
    )(core, updates, updates, updates, warped, field, halo_warped, halo_field, halo_current)


def last_kernel(
    core_ref,
    warped_ref,
    field_ref,
    mine_ref,
    other_ref,
    old_warped_ref,
    old_field_ref,
    halo_warped_ref,
    halo_field_ref,
    moved_ref,
    keep_ref,
    send_ref,
    ring,
):
    subj_dev, block, plane, depth = warped_ref.shape
    step, steps = pl.program_id(0), pl.num_programs(0)
    blocks = steps - 1
    core = core_ref[0]
    halves = edges((plane, depth), 0.5)

    def current_at(row):
        mine, other = mine_ref[row].astype(jnp.float32), other_ref[row].astype(jnp.float32)
        low = jnp.where(core == 0, mine, other)
        high = jnp.where(core == 0, other, mine)
        return jnp.concatenate([low, high], axis=0)

    def halo_update(h, row, place):
        current = current_at(row)
        for s in range(subj_dev):
            f = [halo_field_ref[c, s, h] for c in range(3)]
            u = update_of(halo_warped_ref[s, h + 1], f, current, halves)
            for c in range(3):
                ring[c, s, place] = u[c]

    @pl.when(step == 0)
    def _():
        halo_update(0, 0, block)

    @pl.when(step < blocks)
    def _():
        def tile(r, carry):
            current = current_at(step * block + r + 1)
            for s in range(subj_dev):
                f = [field_ref[c, s, r] for c in range(3)]
                u = update_of(warped_ref[s, r], f, current, halves)
                for c in range(3):
                    ring[c, s, block + 1 + r] = u[c]
            return carry

        lax.fori_loop(0, block, tile, 0, unroll=4)

    @pl.when(step == blocks)
    def _():
        halo_update(1, blocks * block + 1, block + 1)

    @pl.when(step > 0)
    def _():
        def tile(r, carry):
            total = None
            for s in range(subj_dev):
                w = old_warped_ref[s, r]
                g = slopes(w, halves)
                f = []
                for c in range(3):
                    delta = smooth(ring[c, s, r], ring[c, s, r + 1], ring[c, s, r + 2], halves)
                    f.append(old_field_ref[c, s, r] - delta)
                    moved_ref[c, s, r] = f[c]
                p = predict(w, g, f)
                total = p if total is None else total + p
            quarter = plane // 4
            low, high = total[: 2 * quarter], total[2 * quarter :]
            upper = lax.broadcasted_iota(jnp.int32, low.shape, 0) >= quarter
            even = jnp.where(upper, pltpu.roll(high, quarter, 0), low)
            odd = jnp.where(upper, high, pltpu.roll(low, quarter, 0))
            row = (step - 1) * block + r
            keep_ref[row] = jnp.where(core == 0, even, odd)
            send_ref[row] = jnp.where(core == 0, odd, even)
            return carry

        lax.fori_loop(0, block, tile, 0, unroll=2)

    for c in range(3):
        for s in range(subj_dev):
            for r in range(block + 1):
                ring[c, s, r] = ring[c, s, block + r]


def last(core, warped, field, mine, other, halo_warped, halo_field):
    _, subj_dev, rows, plane, depth = field.shape
    blocks = rows // BLOCK
    now = lambda i: jnp.minimum(i, blocks - 1)
    old = lambda i: jnp.maximum(i - 1, 0)
    five = (3, subj_dev, BLOCK, plane, depth)
    four = (subj_dev, BLOCK, plane, depth)
    sums = jax.ShapeDtypeStruct((rows, plane // 2, depth), jnp.float32)
    return pl.pallas_call(
        last_kernel,
        grid=(blocks + 1,),
        out_shape=(jax.ShapeDtypeStruct(field.shape, jnp.float32), sums, sums),
        in_specs=[
            SMEM,
            pl.BlockSpec(four, lambda i: (0, now(i), 0, 0)),
            pl.BlockSpec(five, lambda i: (0, 0, now(i), 0, 0)),
            VMEM,
            VMEM,
            pl.BlockSpec(four, lambda i: (0, old(i), 0, 0)),
            pl.BlockSpec(five, lambda i: (0, 0, old(i), 0, 0)),
            VMEM,
            VMEM,
        ],
        out_specs=(
            pl.BlockSpec(five, lambda i: (0, 0, old(i), 0, 0)),
            pl.BlockSpec(sums.shape, lambda i: (0, 0, 0)),
            pl.BlockSpec(sums.shape, lambda i: (0, 0, 0)),
        ),
        scratch_shapes=[pltpu.VMEM((3, subj_dev, 2 * BLOCK + 1, plane, depth), jnp.float32)],
        compiler_params=params(),
        name="last",
    )(core, warped, field, mine, other, warped, field, halo_warped, halo_field)


def swap(value, axis, mask):
    count = lax.axis_size(axis)
    return lax.ppermute(value, axis, [(i, i ^ mask) for i in range(count)])


def halo(low_rows, high_rows, dim):
    count = lax.axis_size("space")
    forward = [(i, i + 1) for i in range(count - 1)]
    backward = [(i + 1, i) for i in range(count - 1)]
    before = lax.ppermute(high_rows, "space", forward)
    after = lax.ppermute(low_rows, "space", backward)
    return jnp.concatenate([before, after], axis=dim)


def body(images, velocity, weights, template, owners, local_rows, tile_counts):
    spaces = lax.axis_size("space")
    groups = lax.axis_size("subj")
    subj_dev, rows, plane, depth = images.shape
    cap = subj_dev * (2 * rows // spaces)
    subjects = subj_dev * groups
    position = lax.axis_index("subj")
    core = lax.rem(position, 2)[None]
    me = lax.axis_index("space")[None]

    request, slots = plan(tile_counts, owners, local_rows, cap, spaces)
    wanted = lax.all_to_all(request, "space", split_axis=0, concat_axis=0, tiled=True)

    halo_field = halo(velocity[:, :, :2], velocity[:, :, rows - 2 :], 2)
    halo_template = halo(template[:2], template[rows - 2 :], 0)
    ends = jnp.concatenate([template, halo_template], axis=0)
    shares = jnp.stack([ends] + [swap(ends, "subj", k) for k in range(1, groups)])
    order = lax.bitwise_xor(jnp.arange(groups, dtype=jnp.int32), position)
    whole = jnp.moveaxis(shares[order], 0, 1).reshape(rows + 4, plane, depth)

    sends = pick(me, wanted, images.reshape(subj_dev * rows, plane, depth), cap)
    parts = [sends[0]] + [swap(sends[k], "space", k) for k in range(1, spaces)]
    warped, low, high = warp(me, tile_counts, slots, parts, weights)
    halo_warped = halo(low, high, 1)

    updates = update(warped, velocity, whole)
    field, halo_moved, keep, send = move(
        core, updates, warped, velocity, halo_warped, halo_field, whole[rows:]
    )
    share = keep + swap(send, "subj", 1)
    mask = 2
    while mask < groups:
        share = share + swap(share.astype(jnp.bfloat16), "subj", mask).astype(jnp.float32)
        mask = 2 * mask
    mine = (share / subjects).astype(jnp.bfloat16)
    other = swap(mine, "subj", 1)

    field, keep, send = last(core, warped, field, mine, other, halo_warped, halo_moved)
    if groups == 4:
        share = keep + swap(send, "subj", 1)
        chip = lax.div(position, 2)
        quarter = plane // groups
        own = lax.dynamic_slice_in_dim(share, chip * quarter, quarter, 1)
        away = lax.dynamic_slice_in_dim(share, (1 - chip) * quarter, quarter, 1)
        result = (own + swap(away, "subj", 2)) / subjects
    else:
        quarter = plane // 4
        even = jnp.where(core[0] == 0, keep, send)
        odd = jnp.where(core[0] == 0, send, keep)
        total = jnp.concatenate(
            [even[:, :quarter], odd[:, :quarter], even[:, quarter:], odd[:, quarter:]], axis=1
        )
        result = lax.psum_scatter(total, "subj", scatter_dimension=1, tiled=True) / subjects
    return field, result


def solution(mesh):
    in_specs = (
        P("subj", "space", None, None),
        P(None, "subj", "space", None, None),
        P(None, "subj", "space", None, None),
        P("space", "subj", None),
        P("subj", "space", None),
        P("subj", "space"),
        P("subj", "space"),
    )
    out_specs = (P(None, "subj", "space", None, None), P("space", "subj", None))
    return jax.shard_map(body, mesh=mesh, in_specs=in_specs, out_specs=out_specs, check_vma=False)
```

time: 180 us -> 109 us (0.61)
  waiting for transfers between devices: 63.3 us -> 21.7 us
  starting transfers between devices: 13.8 us -> 48.5 us
  other arithmetic: 30.6 us -> 0.97 us
  Pallas kernels: 0 us -> 26.9 us
  blocking collectives: 26.5 us -> 0 us
  local copies, waits for them, and re-layouts: 30.8 us -> 9.92 us
  between operations: 14.5 us -> 0.91 us
    reduce_scatter x2 -> x0, waiting for transfers between devices: 42.3 us -> none  [body(): lax.psum_scatter(local_sum, 'subj', scatter_dimension=1, tiled=True)]
    ppermute x4 -> x21, starting transfers between devices: 9.5 us -> 42.3 us  [the longest x15 23.4 us: swap(): return lax.ppermute(value, axis, [(i, i ^ mask) for i in range(count)])]
    pallas_call x0 -> x6, Pallas kernels: none -> 26.9 us  [the longest x1 8.63 us: last(): pl.pallas_call(last_kernel, grid=(blocks + 1,), out_shape=(jax.ShapeDtype...]
    all_to_all x1 -> x0, blocking collectives: 13.6 us -> none  [body(): lax.all_to_all(request, 'space', split_axis=1, concat_axis=1, tiled=True)]
    all_gather x2 -> x0, blocking collectives: 13 us -> none  [the longest x1 7.17 us: body(): whole = lax.all_gather(template, 'subj', axis=1, tiled=True)]
    ppermute x4 -> x21, waiting for transfers between devices: 8.97 us -> 21.7 us  [the longest x15 21.7 us: swap(): return lax.ppermute(value, axis, [(i, i ^ mask) for i in range(count)])]
    all_to_all x1, waiting for transfers between devices: 11.9 us -> 0.01 us  [body(): lax.all_to_all(request, 'space', split_axis=0, concat_axis=0, tiled=True)]
    slice x15 -> x4, local copies, waits for them, and re-layouts: 11.5 us -> 1.67 us  [the longest x1 0.96 us: body(): halo_field = halo(velocity[:, :, :2], velocity[:, :, rows - 2:], 2)]
  transfers between devices with their start and end apart: 7 -> 22, of which waited for: 7 -> 10; matrix products, arithmetic and copies ran while one was open for 3% -> 4% of each run, Pallas kernels for 0% -> 10%
where the time goes in v1:
time: 109 us
  starting transfers between devices  48.5 us (44%)
  Pallas kernels  26.9 us (25%)
  waiting for transfers between devices  21.7 us (20%)
  local copies, waits for them, and re-layouts  9.92 us (9%)
    ppermute x15, starting transfers between devices, swap(): return lax.ppermute(value, axis, [(i, i ^ mask) for i in range(count)])  23.4 us
    ppermute x15, waiting for transfers between devices, swap(): return lax.ppermute(value, axis, [(i, i ^ mask) for i in range(count)])  21.7 us
    ppermute x3, starting transfers between devices, halo(): before = lax.ppermute(high_rows, 'space', forward)  15 us
    pallas_call x1, Pallas kernels, last(): pl.pallas_call(last_kernel, grid=(blocks + 1,), out_shape=(jax.ShapeDtype...  8.63 us
    unnamed x13, local copies, waits for them, and re-layouts  7.22 us
    pallas_call x1, Pallas kernels, move(): pl.pallas_call(move_kernel, grid=(rows // BLOCK,), out_shape=(jax.ShapeDt...  7.13 us
    all_to_all x1, starting transfers between devices, body(): lax.all_to_all(request, 'space', split_axis=0, concat_axis=0, tiled=True)  6.22 us
    pallas_call x1, Pallas kernels, warp(): pl.pallas_call(functools.partial(warp_kernel, spaces), grid=(rows // BLOC...  4.57 us
  transfers between devices with their start and end apart: 22, of which 10 were waited for; matrix products, arithmetic and copies ran while one was open for 4% of the time, Pallas kernels for 10%

profile of v1, /device:TPU:0, one launch (start us, length us, event | category | flops | bytes accessed | tf_op | source)
XLA Modules:
  0.0 108.9 jit_solution(8510121431325646771)
XLA Ops:
  0.6 0.7 fusion.3
  1.3 1.3 %collective-permute-start.8 = (f32[2,4,128]{2,1,0:T(4,128)S(1)}, f32[2,4,128]{2,1,0:T(4,128)S(1)}, u32[]{:S(2)}, u32[]{:S(2)}) collective-permute-start(f32[2,4,128]{2,1,0:T(4,128)S(1)} %get-tuple-element.46), channel_id=1, source_target_pairs={{1,0},{2,1},{3,2},{4,3},{5,4},{6,5},{7,6},{9,8},{10,9},{11,10},{12... | collective-permute-start | bytes 12296 | tf_op jit(solution)/shard_map/ppermute | solution.py:579
  2.6 5.5 %collective-permute-start.7 = (f32[2,4,128]{2,1,0:T(4,128)S(1)}, f32[2,4,128]{2,1,0:T(4,128)S(1)}, u32[]{:S(2)}, u32[]{:S(2)}) collective-permute-start(f32[2,4,128]{2,1,0:T(4,128)S(1)} %get-tuple-element.47), channel_id=1, source_target_pairs={{0,1},{1,2},{2,3},{3,4},{4,5},{5,6},{6,7},{8,9},{9,10},{10,11},{11... | collective-permute-start | bytes 12296 | tf_op jit(solution)/shard_map/ppermute | solution.py:578
  8.1 0.7 copy.17.counts_ref
  8.9 0.8 copy.15.owners_ref
  9.7 0.0 copy-start.3
  9.7 0.7 copy-done.3
  10.3 1.6 %plan.1 = (s32[8,128]{1,0:T(8,128)}, s32[2,64]{1,0:T(2,128)S(1)}) custom-call(s32[2,1]{1,0:T(2,128)S(1)} %copy.17.counts_ref, s32[2,64,1]{2,1,0:T(8,128)S(1)} %copy.15.owners_ref, s32[2,64]{1,0:T(2,128)S(1)} %copy-done.3), custom_call_target="tpu_custom_call" | custom-call | tf_op jit(solution)/shard_map/plan/pallas_call | solution.py:83
  12.0 6.2 %all-to-all-start = ((s32[8,1,128]{2,1,0:T(1,128)}), s32[8,1,128]{2,1,0:T(1,128)S(1)}, u32[]{:S(2)}, u32[]{:S(2)}) async-start(s32[8,1,128]{2,1,0:T(1,128)} %bitcast.3), calls=%async_computation | async-start | bytes 8192 | tf_op jit(solution)/shard_map/all_to_all | solution.py:594
  18.2 1.0 fusion.2
  19.1 3.9 %collective-permute-start.14 = (f32[3,2,2,16,128]{4,3,2,1,0:T(8,128)S(1)}, f32[3,2,2,16,128]{4,3,2,1,0:T(8,128)S(1)}, u32[]{:S(2)}, u32[]{:S(2)}) collective-permute-start(f32[3,2,2,16,128]{4,3,2,1,0:T(8,128)S(1)} %get-tuple-element.44), channel_id=1, source_target_pairs={{0,1},{1,2},{2,3},{3,4},{4,5},{5,6},{6,7},{8,9},{9,10},{10,11},{11... | collective-permute-start | bytes 294920 | tf_op jit(solution)/shard_map/ppermute | solution.py:578
  23.1 1.3 %collective-permute-start.15 = (f32[3,2,2,16,128]{4,3,2,1,0:T(8,128)S(1)}, f32[3,2,2,16,128]{4,3,2,1,0:T(8,128)S(1)}, u32[]{:S(2)}, u32[]{:S(2)}) collective-permute-start(f32[3,2,2,16,128]{4,3,2,1,0:T(8,128)S(1)} %get-tuple-element.45), channel_id=1, source_target_pairs={{1,0},{2,1},{3,2},{4,3},{5,4},{6,5},{7,6},{9,8},{10,9},{11,10},{12... | collective-permute-start | bytes 294920 | tf_op jit(solution)/shard_map/ppermute | solution.py:579
  24.4 0.9 constant_dynamic-update-slice_fusion.2
  25.3 0.0 all-to-all-done
  25.3 0.0 copy-start.2
  25.3 1.0 copy-done.2
  26.4 0.9 pick.1
  27.2 2.7 %collective-permute-start = (bf16[32,16,128]{2,1,0:T(8,128)(2,1)S(1)}, bf16[32,16,128]{2,1,0:T(8,128)(2,1)S(1)}, u32[]{:S(2)}, u32[]{:S(2)}) collective-permute-start(bf16[32,16,128]{2,1,0:T(8,128)(2,1)S(1)} %get-tuple-element.25), channel_id=1, source_target_pairs={{0,1},{1,0},{2,3},{3,2},{4,5},{5,4},{6,7},{7,6},{8,9},{9,8},{10,11... | collective-permute-start | bytes 393224 | tf_op jit(solution)/shard_map/ppermute | solution.py:571
  30.0 0.0 collective-permute-done.8
  30.0 1.5 %collective-permute-start.1 = (bf16[32,16,128]{2,1,0:T(8,128)(2,1)S(1)}, bf16[32,16,128]{2,1,0:T(8,128)(2,1)S(1)}, u32[]{:S(2)}, u32[]{:S(2)}) collective-permute-start(bf16[32,16,128]{2,1,0:T(8,128)(2,1)S(1)} %get-tuple-element.26), channel_id=1, source_target_pairs={{0,2},{1,3},{2,0},{3,1},{4,6},{5,7},{6,4},{7,5},{8,10},{9,11},{10,... | collective-permute-start | bytes 393224 | tf_op jit(solution)/shard_map/ppermute | solution.py:571
  31.4 0.0 collective-permute-done.7
  31.4 1.0 collective-permute-start.2
  32.4 0.0 collective-permute-done.14
  32.4 2.9 %collective-permute-start.3 = (bf16[32,16,128]{2,1,0:T(8,128)(2,1)S(1)}, bf16[32,16,128]{2,1,0:T(8,128)(2,1)S(1)}, u32[]{:S(2)}, u32[]{:S(2)}) collective-permute-start(bf16[32,16,128]{2,1,0:T(8,128)(2,1)S(1)} %get-tuple-element.28), channel_id=1, source_target_pairs={{0,4},{1,5},{2,6},{3,7},{4,0},{5,1},{6,2},{7,3},{8,12},{9,13},{10,... | collective-permute-start | bytes 393224 | tf_op jit(solution)/shard_map/ppermute | solution.py:571
  35.3 0.0 collective-permute-done.15
  35.3 0.6 collective-permute-start.4
  35.8 0.0 collective-permute-done.refs_1_
  35.8 0.1 collective-permute-start.11
  35.9 2.2 %collective-permute-done.1.refs_2_ = bf16[32,16,128]{2,1,0:T(8,128)(2,1)S(1)} collective-permute-done((bf16[32,16,128]{2,1,0:T(8,128)(2,1)S(1)}, bf16[32,16,128]{2,1,0:T(8,128)(2,1)S(1)}, u32[]{:S(2)}, u32[]{:S(2)}) %collective-permute-start.1) | collective-permute-done | bytes 131104 | tf_op jit(solution)/shard_map/ppermute | solution.py:571
  38.1 1.5 %collective-permute-start.10 = (f32[68,4,128]{2,1,0:T(4,128)S(1)}, f32[68,4,128]{2,1,0:T(4,128)S(1)}, u32[]{:S(2)}, u32[]{:S(2)}) collective-permute-start(f32[68,4,128]{2,1,0:T(4,128)S(1)} %constant_dynamic-update-slice_fusion), channel_id=1, source_target_pairs={{0,16},{8,24},{16,0},{24,8},{1,17},{9,25},{17,1},{25,9},{2,18},{10... | collective-permute-start | bytes 417800 | tf_op jit(solution)/shard_map/ppermute | solution.py:571
  39.6 0.1 collective-permute-done.2.refs_3_
  39.7 0.0 collective-permute-start.9
  39.7 1.3 %collective-permute-done.3.refs_4_ = bf16[32,16,128]{2,1,0:T(8,128)(2,1)S(1)} collective-permute-done((bf16[32,16,128]{2,1,0:T(8,128)(2,1)S(1)}, bf16[32,16,128]{2,1,0:T(8,128)(2,1)S(1)}, u32[]{:S(2)}, u32[]{:S(2)}) %collective-permute-start.3) | collective-permute-done | bytes 131104 | tf_op jit(solution)/shard_map/ppermute | solution.py:571
  41.0 6.3 %collective-permute-start.5 = (bf16[32,16,128]{2,1,0:T(8,128)(2,1)S(1)}, bf16[32,16,128]{2,1,0:T(8,128)(2,1)S(1)}, u32[]{:S(2)}, u32[]{:S(2)}) collective-permute-start(bf16[32,16,128]{2,1,0:T(8,128)(2,1)S(1)} %get-tuple-element.30), channel_id=1, source_target_pairs={{0,6},{1,7},{2,4},{3,5},{4,2},{5,3},{6,0},{7,1},{8,14},{9,15},{10,... | collective-permute-start | bytes 393224 | tf_op jit(solution)/shard_map/ppermute | solution.py:571
  47.3 1.5 %collective-permute-done.4.refs_5_ = bf16[32,16,128]{2,1,0:T(8,128)(2,1)S(1)} collective-permute-done((bf16[32,16,128]{2,1,0:T(8,128)(2,1)S(1)}, bf16[32,16,128]{2,1,0:T(8,128)(2,1)S(1)}, u32[]{:S(2)}, u32[]{:S(2)}) %collective-permute-start.4) | collective-permute-done | bytes 131104 | tf_op jit(solution)/shard_map/ppermute | solution.py:571
  48.8 3.6 %collective-permute-start.6 = (bf16[32,16,128]{2,1,0:T(8,128)(2,1)S(1)}, bf16[32,16,128]{2,1,0:T(8,128)(2,1)S(1)}, u32[]{:S(2)}, u32[]{:S(2)}) collective-permute-start(bf16[32,16,128]{2,1,0:T(8,128)(2,1)S(1)} %get-tuple-element.31), channel_id=1, source_target_pairs={{0,7},{1,6},{2,5},{3,4},{4,3},{5,2},{6,1},{7,0},{8,15},{9,14},{10,... | collective-permute-start | bytes 393224 | tf_op jit(solution)/shard_map/ppermute | solution.py:571
  52.4 0.0 collective-permute-done.5.refs_6_
  52.4 4.1 %collective-permute-done.6.refs_7_ = bf16[32,16,128]{2,1,0:T(8,128)(2,1)S(1)} collective-permute-done((bf16[32,16,128]{2,1,0:T(8,128)(2,1)S(1)}, bf16[32,16,128]{2,1,0:T(8,128)(2,1)S(1)}, u32[]{:S(2)}, u32[]{:S(2)}) %collective-permute-start.6) | collective-permute-done | bytes 131104 | tf_op jit(solution)/shard_map/ppermute | solution.py:571
  56.6 1.4 %copy-done.1 = bf16[3,2,64,16,128]{4,3,2,1,0:T(8,128)(2,1)S(1)} copy-done((bf16[3,2,64,16,128]{4,3,2,1,0:T(8,128)(2,1)S(1)}, bf16[3,2,64,16,128]{4,3,2,1,0:T(8,128)(2,1)}, u32[]{:S(2)}) %copy-start.1) | copy-done | bytes 1572888
  58.0 4.6 %warp.1 = (f32[2,64,16,128]{3,2,1,0:T(8,128)S(1)}, f32[2,2,16,128]{3,2,1,0:T(8,128)S(1)}, f32[2,2,16,128]{3,2,1,0:T(8,128)S(1)}) custom-call(s32[1]{0:T(128)} %bitcast.1.me_ref, s32[2,1]{1,0:T(2,128)S(1)} %copy.17.counts_ref, s32[2,64]{1,0:T(2,128)S(1)} %get-tuple-element.22.slots_ref, bf16[32,16,128]{2,1,0:T(8,128)(2,1)S(1)} %get-tuple-element.24.refs_0_, ...), custom_call_target="tpu_custom_call" | custom-call | tf_op jit(solution)/shard_map/warp/pallas_call | solution.py:224
  62.6 5.6 %collective-permute-start.12 = (f32[2,2,16,128]{3,2,1,0:T(8,128)S(1)}, f32[2,2,16,128]{3,2,1,0:T(8,128)S(1)}, u32[]{:S(2)}, u32[]{:S(2)}) collective-permute-start(f32[2,2,16,128]{3,2,1,0:T(8,128)S(1)} %get-tuple-element.33), channel_id=1, source_target_pairs={{0,1},{1,2},{2,3},{3,4},{4,5},{5,6},{6,7},{8,9},{9,10},{10,11},{11... | collective-permute-start | bytes 98312 | tf_op jit(solution)/shard_map/ppermute | solution.py:578
  68.1 1.3 %collective-permute-start.13 = (f32[2,2,16,128]{3,2,1,0:T(8,128)S(1)}, f32[2,2,16,128]{3,2,1,0:T(8,128)S(1)}, u32[]{:S(2)}, u32[]{:S(2)}) collective-permute-start(f32[2,2,16,128]{3,2,1,0:T(8,128)S(1)} %get-tuple-element.34), channel_id=1, source_target_pairs={{1,0},{2,1},{3,2},{4,3},{5,4},{6,5},{7,6},{9,8},{10,9},{11,10},{12... | collective-permute-start | bytes 98312 | tf_op jit(solution)/shard_map/ppermute | solution.py:579
  69.4 0.0 collective-permute-done.11
  69.4 0.0 collective-permute-done.10
  69.4 0.0 collective-permute-done.9
  69.5 0.1 pad_maximum_fusion
  69.6 0.9 gather_fusion
  70.5 0.1 copy.18
  70.6 4.0 %update.1.update_ref.before_ref.after_ref = f32[3,2,64,16,128]{4,3,2,1,0:T(8,128)S(1)} custom-call(f32[2,64,16,128]{3,2,1,0:T(8,128)S(1)} %get-tuple-element.32.warped_ref.old_warped_ref, f32[3,2,64,16,128]{4,3,2,1,0:T(8,128)} %field_ref.3, f32[68,16,128]{2,1,0:T(8,128)S(1)} %bitcast.16), custom_call_target="tpu_custom_call" | custom-call | tf_op jit(solution)/shard_map/update/pallas_call | solution.py:291
  74.7 0.0 copy-start
  74.7 1.7 %copy-done = f32[3,2,64,16,128]{4,3,2,1,0:T(8,128)} copy-done((f32[3,2,64,16,128]{4,3,2,1,0:T(8,128)}, f32[3,2,64,16,128]{4,3,2,1,0:T(8,128)S(1)}, u32[]{:S(2)}) %copy-start) | copy-done | bytes 3145752
  76.4 7.1 %move.1 = (f32[3,2,64,16,128]{4,3,2,1,0:T(8,128)S(1)}, f32[3,2,2,16,128]{4,3,2,1,0:T(8,128)S(1)}, f32[66,8,128]{2,1,0:T(8,128)S(1)}, f32[66,8,128]{2,1,0:T(8,128)S(1)}) custom-call(s32[1]{0:T(128)} %bitcast.core_ref, f32[3,2,64,16,128]{4,3,2,1,0:T(8,128)} %copy-done, f32[3,2,64,16,128]{4,3,2,1,0:T(8,128)} %copy-done, f32[3,2,64,16,128]{4,3,2,1,0:T(8,128)} %copy-done, ...), custom_call_target="tpu_custom_call" | custom-call | tf_op jit(solution)/shard_map/move/pallas_call | solution.py:415
  83.5 0.1 collective-permute-start.16
  83.6 1.5 %collective-permute-done.16 = f32[66,8,128]{2,1,0:T(8,128)S(1)} collective-permute-done((f32[66,8,128]{2,1,0:T(8,128)S(1)}, f32[66,8,128]{2,1,0:T(8,128)S(1)}, u32[]{:S(2)}, u32[]{:S(2)}) %collective-permute-start.16) | collective-permute-done | bytes 270368 | tf_op jit(solution)/shard_map/ppermute | solution.py:571
  85.2 1.6 %collective-permute-start.17 = (bf16[66,8,128]{2,1,0:T(8,128)(2,1)S(1)}, bf16[66,8,128]{2,1,0:T(8,128)(2,1)S(1)}, u32[]{:S(2)}, u32[]{:S(2)}) collective-permute-start(bf16[66,8,128]{2,1,0:T(8,128)(2,1)S(1)} %get-tuple-element.42), channel_id=1, source_target_pairs={{0,16},{8,24},{16,0},{24,8},{1,17},{9,25},{17,1},{25,9},{2,18},{10... | collective-permute-start | bytes 405512 | tf_op jit(solution)/shard_map/ppermute | solution.py:571
  86.7 4.1 %collective-permute-done.17 = bf16[66,8,128]{2,1,0:T(8,128)(2,1)S(1)} collective-permute-done((bf16[66,8,128]{2,1,0:T(8,128)(2,1)S(1)}, bf16[66,8,128]{2,1,0:T(8,128)(2,1)S(1)}, u32[]{:S(2)}, u32[]{:S(2)}) %collective-permute-start.17) | collective-permute-done | bytes 135200 | tf_op jit(solution)/shard_map/ppermute | solution.py:571
  90.9 0.1 collective-permute-start.18
  91.0 1.3 %collective-permute-done.18.other_ref = bf16[66,8,128]{2,1,0:T(8,128)(2,1)S(1)} collective-permute-done((bf16[66,8,128]{2,1,0:T(8,128)(2,1)S(1)}, bf16[66,8,128]{2,1,0:T(8,128)(2,1)S(1)}, u32[]{:S(2)}, u32[]{:S(2)}) %collective-permute-start.18) | collective-permute-done | bytes 135200 | tf_op jit(solution)/shard_map/ppermute | solution.py:571
  92.3 8.6 %last.1 = (f32[3,2,64,16,128]{4,3,2,1,0:T(8,128)}, f32[64,8,128]{2,1,0:T(8,128)S(1)}, f32[64,8,128]{2,1,0:T(8,128)S(1)}) custom-call(s32[1]{0:T(128)} %bitcast.core_ref, f32[2,64,16,128]{3,2,1,0:T(8,128)S(1)} %get-tuple-element.32.warped_ref.old_warped_ref, f32[3,2,64,16,128]{4,3,2,1,0:T(8,128)S(1)} %get-tuple-element.35.field_ref.old_field_ref, ...), custom_call_target="tpu_custom_call" | custom-call | tf_op jit(solution)/shard_map/last/pallas_call | solution.py:543
  100.9 0.1 collective-permute-start.19
  101.1 1.4 %collective-permute-done.19 = f32[64,8,128]{2,1,0:T(8,128)S(1)} collective-permute-done((f32[64,8,128]{2,1,0:T(8,128)S(1)}, f32[64,8,128]{2,1,0:T(8,128)S(1)}, u32[]{:S(2)}, u32[]{:S(2)}) %collective-permute-start.19) | collective-permute-done | bytes 262176 | tf_op jit(solution)/shard_map/ppermute | solution.py:571
  102.5 1.6 %collective-permute-start.20 = (f32[64,4,128]{2,1,0:T(4,128)S(1)}, f32[64,4,128]{2,1,0:T(4,128)S(1)}, u32[]{:S(2)}, u32[]{:S(2)}) collective-permute-start(f32[64,4,128]{2,1,0:T(4,128)S(1)} %constant_dynamic-slice_fusion), channel_id=1, source_target_pairs={{0,16},{8,24},{16,0},{24,8},{1,17},{9,25},{17,1},{25,9},{2,18},{10... | collective-permute-start | bytes 393224 | tf_op jit(solution)/shard_map/ppermute | solution.py:571
  104.1 4.1 %collective-permute-done.20 = f32[64,4,128]{2,1,0:T(4,128)S(1)} collective-permute-done((f32[64,4,128]{2,1,0:T(4,128)S(1)}, f32[64,4,128]{2,1,0:T(4,128)S(1)}, u32[]{:S(2)}, u32[]{:S(2)}) %collective-permute-start.20) | collective-permute-done | bytes 131104 | tf_op jit(solution)/shard_map/ppermute | solution.py:571
  108.2 0.7 add_multiply_fusion
  (16 shorter events, 0.2 us)
Async XLA Ops:
  1.3 28.6 %collective-permute-start.8 = (f32[2,4,128]{2,1,0:T(4,128)S(1)}, f32[2,4,128]{2,1,0:T(4,128)S(1)}, u32[]{:S(2)}, u32[]{:S(2)}) collective-permute-start(f32[2,4,128]{2,1,0:T(4,128)S(1)} %get-tuple-element.46), channel_id=1, source_target_pairs={{1,0},{2,1},{3,2},{4,3},{5,4},{6,5},{7,6},{9,8},{10,9},{11,10},{12... | collective-permute-start | bytes 12296 | tf_op jit(solution)/shard_map/ppermute | solution.py:579
  2.6 28.8 %collective-permute-start.7 = (f32[2,4,128]{2,1,0:T(4,128)S(1)}, f32[2,4,128]{2,1,0:T(4,128)S(1)}, u32[]{:S(2)}, u32[]{:S(2)}) collective-permute-start(f32[2,4,128]{2,1,0:T(4,128)S(1)} %get-tuple-element.47), channel_id=1, source_target_pairs={{0,1},{1,2},{2,3},{3,4},{4,5},{5,6},{6,7},{8,9},{9,10},{10,11},{11... | collective-permute-start | bytes 12296 | tf_op jit(solution)/shard_map/ppermute | solution.py:578
  9.7 0.7 copy-start.3
  12.0 13.4 %all-to-all-start = ((s32[8,1,128]{2,1,0:T(1,128)}), s32[8,1,128]{2,1,0:T(1,128)S(1)}, u32[]{:S(2)}, u32[]{:S(2)}) async-start(s32[8,1,128]{2,1,0:T(1,128)} %bitcast.3), calls=%async_computation | async-start | bytes 8192 | tf_op jit(solution)/shard_map/all_to_all | solution.py:594
  19.1 13.3 %collective-permute-start.14 = (f32[3,2,2,16,128]{4,3,2,1,0:T(8,128)S(1)}, f32[3,2,2,16,128]{4,3,2,1,0:T(8,128)S(1)}, u32[]{:S(2)}, u32[]{:S(2)}) collective-permute-start(f32[3,2,2,16,128]{4,3,2,1,0:T(8,128)S(1)} %get-tuple-element.44), channel_id=1, source_target_pairs={{0,1},{1,2},{2,3},{3,4},{4,5},{5,6},{6,7},{8,9},{9,10},{10,11},{11... | collective-permute-start | bytes 294920 | tf_op jit(solution)/shard_map/ppermute | solution.py:578
  23.1 12.2 %collective-permute-start.15 = (f32[3,2,2,16,128]{4,3,2,1,0:T(8,128)S(1)}, f32[3,2,2,16,128]{4,3,2,1,0:T(8,128)S(1)}, u32[]{:S(2)}, u32[]{:S(2)}) collective-permute-start(f32[3,2,2,16,128]{4,3,2,1,0:T(8,128)S(1)} %get-tuple-element.45), channel_id=1, source_target_pairs={{1,0},{2,1},{3,2},{4,3},{5,4},{6,5},{7,6},{9,8},{10,9},{11,10},{12... | collective-permute-start | bytes 294920 | tf_op jit(solution)/shard_map/ppermute | solution.py:579
  25.3 1.0 copy-start.2
  27.2 8.6 %collective-permute-start = (bf16[32,16,128]{2,1,0:T(8,128)(2,1)S(1)}, bf16[32,16,128]{2,1,0:T(8,128)(2,1)S(1)}, u32[]{:S(2)}, u32[]{:S(2)}) collective-permute-start(bf16[32,16,128]{2,1,0:T(8,128)(2,1)S(1)} %get-tuple-element.25), channel_id=1, source_target_pairs={{0,1},{1,0},{2,3},{3,2},{4,5},{5,4},{6,7},{7,6},{8,9},{9,8},{10,11... | collective-permute-start | bytes 393224 | tf_op jit(solution)/shard_map/ppermute | solution.py:571
  30.0 8.1 %collective-permute-start.1 = (bf16[32,16,128]{2,1,0:T(8,128)(2,1)S(1)}, bf16[32,16,128]{2,1,0:T(8,128)(2,1)S(1)}, u32[]{:S(2)}, u32[]{:S(2)}) collective-permute-start(bf16[32,16,128]{2,1,0:T(8,128)(2,1)S(1)} %get-tuple-element.26), channel_id=1, source_target_pairs={{0,2},{1,3},{2,0},{3,1},{4,6},{5,7},{6,4},{7,5},{8,10},{9,11},{10,... | collective-permute-start | bytes 393224 | tf_op jit(solution)/shard_map/ppermute | solution.py:571
  31.4 8.2 %collective-permute-start.2 = (bf16[32,16,128]{2,1,0:T(8,128)(2,1)S(1)}, bf16[32,16,128]{2,1,0:T(8,128)(2,1)S(1)}, u32[]{:S(2)}, u32[]{:S(2)}) collective-permute-start(bf16[32,16,128]{2,1,0:T(8,128)(2,1)S(1)} %get-tuple-element.27), channel_id=1, source_target_pairs={{0,3},{1,2},{2,1},{3,0},{4,7},{5,6},{6,5},{7,4},{8,11},{9,10},{10,... | collective-permute-start | bytes 393224 | tf_op jit(solution)/shard_map/ppermute | solution.py:571
  32.4 8.6 %collective-permute-start.3 = (bf16[32,16,128]{2,1,0:T(8,128)(2,1)S(1)}, bf16[32,16,128]{2,1,0:T(8,128)(2,1)S(1)}, u32[]{:S(2)}, u32[]{:S(2)}) collective-permute-start(bf16[32,16,128]{2,1,0:T(8,128)(2,1)S(1)} %get-tuple-element.28), channel_id=1, source_target_pairs={{0,4},{1,5},{2,6},{3,7},{4,0},{5,1},{6,2},{7,3},{8,12},{9,13},{10,... | collective-permute-start | bytes 393224 | tf_op jit(solution)/shard_map/ppermute | solution.py:571
  35.3 13.5 %collective-permute-start.4 = (bf16[32,16,128]{2,1,0:T(8,128)(2,1)S(1)}, bf16[32,16,128]{2,1,0:T(8,128)(2,1)S(1)}, u32[]{:S(2)}, u32[]{:S(2)}) collective-permute-start(bf16[32,16,128]{2,1,0:T(8,128)(2,1)S(1)} %get-tuple-element.29), channel_id=1, source_target_pairs={{0,5},{1,4},{2,7},{3,6},{4,1},{5,0},{6,3},{7,2},{8,13},{9,12},{10,... | collective-permute-start | bytes 393224 | tf_op jit(solution)/shard_map/ppermute | solution.py:571
  35.8 33.6 %collective-permute-start.11 = (f32[68,4,128]{2,1,0:T(4,128)S(1)}, f32[68,4,128]{2,1,0:T(4,128)S(1)}, u32[]{:S(2)}, u32[]{:S(2)}) collective-permute-start(f32[68,4,128]{2,1,0:T(4,128)S(1)} %constant_dynamic-update-slice_fusion), channel_id=1, source_target_pairs={{0,24},{8,16},{16,8},{24,0},{1,25},{9,17},{17,9},{25,1},{2,26},{10... | collective-permute-start | bytes 417800 | tf_op jit(solution)/shard_map/ppermute | solution.py:571
  38.1 31.3 %collective-permute-start.10 = (f32[68,4,128]{2,1,0:T(4,128)S(1)}, f32[68,4,128]{2,1,0:T(4,128)S(1)}, u32[]{:S(2)}, u32[]{:S(2)}) collective-permute-start(f32[68,4,128]{2,1,0:T(4,128)S(1)} %constant_dynamic-update-slice_fusion), channel_id=1, source_target_pairs={{0,16},{8,24},{16,0},{24,8},{1,17},{9,25},{17,1},{25,9},{2,18},{10... | collective-permute-start | bytes 417800 | tf_op jit(solution)/shard_map/ppermute | solution.py:571
  39.7 29.8 %collective-permute-start.9 = (f32[68,4,128]{2,1,0:T(4,128)S(1)}, f32[68,4,128]{2,1,0:T(4,128)S(1)}, u32[]{:S(2)}, u32[]{:S(2)}) collective-permute-start(f32[68,4,128]{2,1,0:T(4,128)S(1)} %constant_dynamic-update-slice_fusion), channel_id=1, source_target_pairs={{0,8},{8,0},{16,24},{24,16},{1,9},{9,1},{17,25},{25,17},{2,10},{10... | collective-permute-start | bytes 417800 | tf_op jit(solution)/shard_map/ppermute | solution.py:571
  41.0 11.5 %collective-permute-start.5 = (bf16[32,16,128]{2,1,0:T(8,128)(2,1)S(1)}, bf16[32,16,128]{2,1,0:T(8,128)(2,1)S(1)}, u32[]{:S(2)}, u32[]{:S(2)}) collective-permute-start(bf16[32,16,128]{2,1,0:T(8,128)(2,1)S(1)} %get-tuple-element.30), channel_id=1, source_target_pairs={{0,6},{1,7},{2,4},{3,5},{4,2},{5,3},{6,0},{7,1},{8,14},{9,15},{10,... | collective-permute-start | bytes 393224 | tf_op jit(solution)/shard_map/ppermute | solution.py:571
  48.8 7.8 %collective-permute-start.6 = (bf16[32,16,128]{2,1,0:T(8,128)(2,1)S(1)}, bf16[32,16,128]{2,1,0:T(8,128)(2,1)S(1)}, u32[]{:S(2)}, u32[]{:S(2)}) collective-permute-start(bf16[32,16,128]{2,1,0:T(8,128)(2,1)S(1)} %get-tuple-element.31), channel_id=1, source_target_pairs={{0,7},{1,6},{2,5},{3,4},{4,3},{5,2},{6,1},{7,0},{8,15},{9,14},{10,... | collective-permute-start | bytes 393224 | tf_op jit(solution)/shard_map/ppermute | solution.py:571
  56.6 1.4 %copy-start.1 = (bf16[3,2,64,16,128]{4,3,2,1,0:T(8,128)(2,1)S(1)}, bf16[3,2,64,16,128]{4,3,2,1,0:T(8,128)(2,1)}, u32[]{:S(2)}) copy-start(bf16[3,2,64,16,128]{4,3,2,1,0:T(8,128)(2,1)} %refs_8_.1) | copy-start | bytes 4718596
  62.6 13.8 %collective-permute-start.12 = (f32[2,2,16,128]{3,2,1,0:T(8,128)S(1)}, f32[2,2,16,128]{3,2,1,0:T(8,128)S(1)}, u32[]{:S(2)}, u32[]{:S(2)}) collective-permute-start(f32[2,2,16,128]{3,2,1,0:T(8,128)S(1)} %get-tuple-element.33), channel_id=1, source_target_pairs={{0,1},{1,2},{2,3},{3,4},{4,5},{5,6},{6,7},{8,9},{9,10},{10,11},{11... | collective-permute-start | bytes 98312 | tf_op jit(solution)/shard_map/ppermute | solution.py:578
  68.1 8.2 %collective-permute-start.13 = (f32[2,2,16,128]{3,2,1,0:T(8,128)S(1)}, f32[2,2,16,128]{3,2,1,0:T(8,128)S(1)}, u32[]{:S(2)}, u32[]{:S(2)}) collective-permute-start(f32[2,2,16,128]{3,2,1,0:T(8,128)S(1)} %get-tuple-element.34), channel_id=1, source_target_pairs={{1,0},{2,1},{3,2},{4,3},{5,4},{6,5},{7,6},{9,8},{10,9},{11,10},{12... | collective-permute-start | bytes 98312 | tf_op jit(solution)/shard_map/ppermute | solution.py:579
  74.7 1.7 %copy-start = (f32[3,2,64,16,128]{4,3,2,1,0:T(8,128)}, f32[3,2,64,16,128]{4,3,2,1,0:T(8,128)S(1)}, u32[]{:S(2)}) copy-start(f32[3,2,64,16,128]{4,3,2,1,0:T(8,128)S(1)} %update.1.update_ref.before_ref.after_ref) | copy-start | bytes 9437188
  83.5 1.6 %collective-permute-start.16 = (f32[66,8,128]{2,1,0:T(8,128)S(1)}, f32[66,8,128]{2,1,0:T(8,128)S(1)}, u32[]{:S(2)}, u32[]{:S(2)}) collective-permute-start(f32[66,8,128]{2,1,0:T(8,128)S(1)} %get-tuple-element.37), channel_id=1, source_target_pairs={{0,8},{8,0},{16,24},{24,16},{1,9},{9,1},{17,25},{25,17},{2,10},{10... | collective-permute-start | bytes 811016 | tf_op jit(solution)/shard_map/ppermute | solution.py:571
  85.2 5.7 %collective-permute-start.17 = (bf16[66,8,128]{2,1,0:T(8,128)(2,1)S(1)}, bf16[66,8,128]{2,1,0:T(8,128)(2,1)S(1)}, u32[]{:S(2)}, u32[]{:S(2)}) collective-permute-start(bf16[66,8,128]{2,1,0:T(8,128)(2,1)S(1)} %get-tuple-element.42), channel_id=1, source_target_pairs={{0,16},{8,24},{16,0},{24,8},{1,17},{9,25},{17,1},{25,9},{2,18},{10... | collective-permute-start | bytes 405512 | tf_op jit(solution)/shard_map/ppermute | solution.py:571
  90.9 1.4 %collective-permute-start.18 = (bf16[66,8,128]{2,1,0:T(8,128)(2,1)S(1)}, bf16[66,8,128]{2,1,0:T(8,128)(2,1)S(1)}, u32[]{:S(2)}, u32[]{:S(2)}) collective-permute-start(bf16[66,8,128]{2,1,0:T(8,128)(2,1)S(1)} %multiply_convert_fusion.mine_ref), channel_id=1, source_target_pairs={{0,8},{8,0},{16,24},{24,16},{1,9},{9,1},{17,25},{25,17},{2,10},{10... | collective-permute-start | bytes 405512 | tf_op jit(solution)/shard_map/ppermute | solution.py:571
  100.9 1.5 %collective-permute-start.19 = (f32[64,8,128]{2,1,0:T(8,128)S(1)}, f32[64,8,128]{2,1,0:T(8,128)S(1)}, u32[]{:S(2)}, u32[]{:S(2)}) collective-permute-start(f32[64,8,128]{2,1,0:T(8,128)S(1)} %get-tuple-element.41), channel_id=1, source_target_pairs={{0,8},{8,0},{16,24},{24,16},{1,9},{9,1},{17,25},{25,17},{2,10},{10... | collective-permute-start | bytes 786440 | tf_op jit(solution)/shard_map/ppermute | solution.py:571
  102.5 5.6 %collective-permute-start.20 = (f32[64,4,128]{2,1,0:T(4,128)S(1)}, f32[64,4,128]{2,1,0:T(4,128)S(1)}, u32[]{:S(2)}, u32[]{:S(2)}) collective-permute-start(f32[64,4,128]{2,1,0:T(4,128)S(1)} %constant_dynamic-slice_fusion), channel_id=1, source_target_pairs={{0,16},{8,24},{16,0},{24,8},{1,17},{9,25},{17,1},{25,9},{2,18},{10... | collective-permute-start | bytes 393224 | tf_op jit(solution)/shard_map/ppermute | solution.py:571
